TPU v7x, 32 devices: a whole 2x2x4 slice. The times are simulated.
32 devices in a mesh: wide: 16 (over z, y, core), narrow: 2 (over x).
Axes of the slice: x: 2, y: 2, z: 4, core: 2. Of those that a mesh axis runs over, the one named last changes fastest.
Arguments:
- tokens: bfloat16 [32, 512, 768], P(('wide', 'narrow')), may hold values from -6 to 6
- lengths: int32 [32], P(('wide', 'narrow')), may hold values from 128 to 512, as said below
- w_qkv: bfloat16 [768, 2304], P('wide'), may hold values from -0.21875 to 0.21875
- w_out: bfloat16 [768, 768], P('wide'), may hold values from -1.75 to 1.75
- w_in: bfloat16 [768, 3072], P('wide'), may hold values from -0.21875 to 0.21875
- w_down: bfloat16 [3072, 768], P('wide'), may hold values from -0.109375 to 0.109375
- norms_biases: bfloat16 [9216], P('wide'), may hold values from -0.4 to 1.6, as said below
- cotangent: bfloat16 [32, 512, 768], P(('wide', 'narrow')), may hold values from -6 to 6
Outputs:
- output: bfloat16 [32, 512, 768], P(('wide', 'narrow'))
- grad_tokens: float32 [32, 512, 768], P(('wide', 'narrow'))
- grad_qkv: float32 [768, 2304], P('wide')
- grad_out: float32 [768, 768], P('wide')
- grad_in: float32 [768, 3072], P('wide')
- grad_down: float32 [3072, 768], P('wide')
- grad_norms_biases: float32 [9216], P('wide')
Inputs may be any that keep to these rules, and one draw needn't show every extreme that they name: `lengths`: the number of real tokens of each sequence; keys at positions at or past it are padding; some sequence has 512 and some has 128. `norms_biases`: the gains g1 and g2 lie within 0.6 and 1.6, the biases and shifts within -0.4 and 0.4.
All inputs are finite; a program needn't handle non-finite values.
Results may differ from a plain program's by a relative error of at most 0.019.
Values may be sent and summed in bfloat16 or wider, within the bound.
A program may use at most 128 MiB of HBM per device.

v0:
```python
import jax
import jax.numpy as jnp
from jax import lax
from jax.sharding import PartitionSpec as P

HEADS = 12


def norm_rows(values, gain_row, shift_row):
    average = jnp.mean(values, -1, keepdims=True)
    centred = values - average
    spread = jnp.mean(centred * centred, -1, keepdims=True)
    return centred * lax.rsqrt(spread + 1e-06) * gain_row + shift_row


def gelu_exact(values):
    return jax.nn.gelu(values, approximate=False)


def column_sum(values):
    return jnp.sum(values.astype(jnp.float32), 0)


def split_vector(vector, model_width, hidden_width):
    segments = [
        vector[position * model_width : (position + 1) * model_width] for position in range(8)
    ]
    return segments + [vector[8 * model_width : 8 * model_width + hidden_width]]


def pair_blocks(projected, head_count):
    row_count = projected.shape[0]
    pair_count = head_count // 2
    pair_width = projected.shape[1] // (3 * pair_count)
    return projected.reshape(row_count, 3, pair_count, pair_width).transpose(2, 1, 0, 3)


def unpair_blocks(blocks):
    pair_count = blocks.shape[0]
    row_count = blocks.shape[2]
    pair_width = blocks.shape[3]
    return blocks.transpose(2, 1, 0, 3).reshape(row_count, 3 * pair_count * pair_width)


def pair_scores(head_block, usable, factor):
    row_count = head_block.shape[1]
    queries = head_block[0].reshape(row_count, 2, -1)
    key_rows = head_block[1].reshape(row_count, 2, -1)
    values = head_block[2].reshape(row_count, 2, -1)
    scores = (
        jnp.einsum("qhd,khd->hqk", queries, key_rows, preferred_element_type=jnp.float32) * factor
    )
    return (queries, key_rows, values, jnp.where(usable[None, None, :], scores, -1000000000.0))


def attention_forward(blocks, usable, factor):

    def one_pair(head_block):
        queries, key_rows, values, scores = pair_scores(head_block, usable, factor)
        highest = jnp.max(scores, -1, keepdims=True)
        raised = jnp.exp(scores - highest)
        summed = jnp.sum(raised, -1, keepdims=True)
        attend = (raised / summed).astype(jnp.bfloat16)
        context = jnp.einsum("hqk,khd->qhd", attend, values, preferred_element_type=jnp.float32)
        return (context.reshape(context.shape[0], -1), highest[..., 0] + jnp.log(summed[..., 0]))

    return lax.map(one_pair, blocks)


def attention_backward(blocks, grad_pairs, log_totals, usable, factor):

    def one_pair(pair_inputs):
        head_block, grad_context, log_total = pair_inputs
        queries, key_rows, values, scores = pair_scores(head_block, usable, factor)
        attend = jnp.exp(scores - log_total[..., None])
        row_count = grad_context.shape[0]
        grad_heads = grad_context.reshape(row_count, 2, -1)
        grad_values = jnp.einsum(
            "hqk,qhd->khd",
            attend.astype(jnp.bfloat16),
            grad_heads,
            preferred_element_type=jnp.float32,
        )
        grad_attend = jnp.einsum(
            "qhd,khd->hqk", grad_heads, values, preferred_element_type=jnp.float32
        )
        grad_scores = attend * (grad_attend - jnp.sum(attend * grad_attend, -1, keepdims=True))
        grad_low = grad_scores.astype(jnp.bfloat16)
        grad_queries = (
            jnp.einsum("hqk,khd->qhd", grad_low, key_rows, preferred_element_type=jnp.float32)
            * factor
        )
        grad_keys = (
            jnp.einsum("hqk,qhd->khd", grad_low, queries, preferred_element_type=jnp.float32)
            * factor
        )
        return jnp.stack(
            [
                grad_queries.reshape(row_count, -1),
                grad_keys.reshape(row_count, -1),
                grad_values.reshape(row_count, -1),
            ]
        )

    return lax.map(one_pair, (blocks, grad_pairs, log_totals))


def layer_forward(inputs, length, weights):
    w_qkv, w_out, w_in, w_down, vector = weights
    row_count, model_width = inputs.shape
    hidden_width = w_in.shape[1]
    params = split_vector(vector.astype(jnp.float32), model_width, hidden_width)
    joined_bias = jnp.concatenate([params[0], jnp.zeros((model_width,), jnp.float32), params[1]])
    projected = (jnp.dot(inputs, w_qkv, preferred_element_type=jnp.float32) + joined_bias).astype(
        jnp.bfloat16
    )
    blocks = pair_blocks(projected, HEADS)
    usable = jnp.arange(row_count) < length
    factor = (model_width // HEADS) ** (-0.5)
    context_pairs, log_totals = attention_forward(blocks, usable, factor)
    context = context_pairs.transpose(1, 0, 2).reshape(row_count, model_width).astype(jnp.bfloat16)
    resid_one = inputs.astype(jnp.float32) + (
        jnp.dot(context, w_out, preferred_element_type=jnp.float32) + params[2]
    )
    normed_one = norm_rows(resid_one, params[3], params[4])
    normed_low = normed_one.astype(jnp.bfloat16)
    pre_act = jnp.dot(normed_low, w_in, preferred_element_type=jnp.float32) + params[8]
    activated = gelu_exact(pre_act).astype(jnp.bfloat16)
    resid_two = normed_one + (
        jnp.dot(activated, w_down, preferred_element_type=jnp.float32) + params[5]
    )
    result = norm_rows(resid_two, params[6], params[7])
    saved = (
        params,
        blocks,
        usable,
        factor,
        log_totals,
        context,
        resid_one,
        normed_low,
        pre_act,
        activated,
        resid_two,
    )
    return (result, saved)


def layer_backward(inputs, length, grad_result, weights):
    w_qkv, w_out, w_in, w_down, vector = weights
    unused_result, saved = layer_forward(inputs, length, weights)
    (
        params,
        blocks,
        usable,
        factor,
        log_totals,
        context,
        resid_one,
        normed_low,
        pre_act,
        activated,
        resid_two,
    ) = saved
    row_count, model_width = inputs.shape
    unused_two, norm_two_back = jax.vjp(norm_rows, resid_two, params[6], params[7])
    grad_two, grad_gain_two, grad_shift_two = norm_two_back(grad_result)
    grad_feed = grad_two.astype(jnp.bfloat16)
    grad_down = jnp.einsum("sf,sd->fd", activated, grad_feed, preferred_element_type=jnp.float32)
    grad_act = jnp.einsum("sd,fd->sf", grad_feed, w_down, preferred_element_type=jnp.float32)
    unused_act, gelu_back = jax.vjp(gelu_exact, pre_act)
    grad_pre = gelu_back(grad_act)[0].astype(jnp.bfloat16)
    grad_in = jnp.einsum("sd,sf->df", normed_low, grad_pre, preferred_element_type=jnp.float32)
    grad_normed = grad_two + jnp.einsum(
        "sf,df->sd", grad_pre, w_in, preferred_element_type=jnp.float32
    )
    unused_one, norm_one_back = jax.vjp(norm_rows, resid_one, params[3], params[4])
    grad_one, grad_gain_one, grad_shift_one = norm_one_back(grad_normed)
    grad_attended = grad_one.astype(jnp.bfloat16)
    grad_out = jnp.einsum("sd,se->de", context, grad_attended, preferred_element_type=jnp.float32)
    grad_context = jnp.einsum(
        "se,de->sd", grad_attended, w_out, preferred_element_type=jnp.float32
    ).astype(jnp.bfloat16)
    grad_pairs = grad_context.reshape(row_count, HEADS // 2, -1).transpose(1, 0, 2)
    grad_blocks = attention_backward(blocks, grad_pairs, log_totals, usable, factor)
    grad_projected = unpair_blocks(grad_blocks).astype(jnp.bfloat16)
    grad_qkv = jnp.einsum("sd,se->de", inputs, grad_projected, preferred_element_type=jnp.float32)
    grad_inputs = grad_one + jnp.einsum(
        "se,de->sd", grad_projected, w_qkv, preferred_element_type=jnp.float32
    )
    projected_sums = column_sum(grad_projected)
    grad_vector = jnp.concatenate(
        [
            projected_sums[:model_width],
            projected_sums[2 * model_width :],
            column_sum(grad_attended),
            grad_gain_one,
            grad_shift_one,
            column_sum(grad_feed),
            grad_gain_two,
            grad_shift_two,
            column_sum(grad_pre),
        ]
    )
    return (grad_inputs, (grad_qkv, grad_out, grad_in, grad_down, grad_vector))


def local(tokens, lengths, w_qkv, w_out, w_in, w_down, norms_biases, cotangent):
    weights = (
        lax.all_gather(w_qkv, "wide", axis=0, tiled=True),
        lax.all_gather(w_out, "wide", axis=0, tiled=True),
        lax.all_gather(w_in, "wide", axis=0, tiled=True),
        lax.all_gather(w_down, "wide", axis=0, tiled=True),
        lax.all_gather(norms_biases, "wide", axis=0, tiled=True),
    )

    def forward_one(sequence):
        return layer_forward(sequence[0], sequence[1], weights)[0].astype(jnp.bfloat16)

    output = lax.map(forward_one, (tokens, lengths))
    second_copy = (
        lax.all_gather(w_qkv, "wide", axis=0, tiled=True),
        lax.all_gather(w_out, "wide", axis=0, tiled=True),
        lax.all_gather(w_in, "wide", axis=0, tiled=True),
        lax.all_gather(w_down, "wide", axis=0, tiled=True),
        lax.all_gather(norms_biases, "wide", axis=0, tiled=True),
    )
    running = tuple((jnp.zeros(member.shape, jnp.float32) for member in second_copy))

    def advance(totals, sequence):
        grad_inputs, gradients = layer_backward(
            sequence[0], sequence[1], sequence[2].astype(jnp.float32), second_copy
        )
        return (jax.tree.map(jnp.add, totals, gradients), grad_inputs)

    totals, grad_tokens = lax.scan(advance, running, (tokens, lengths, cotangent))
    owned_rows = (
        lax.psum_scatter(
            totals[0].astype(jnp.bfloat16), "wide", scatter_dimension=0, tiled=True
        ).astype(jnp.float32),
        lax.psum_scatter(
            totals[1].astype(jnp.bfloat16), "wide", scatter_dimension=0, tiled=True
        ).astype(jnp.float32),
        lax.psum_scatter(
            totals[2].astype(jnp.bfloat16), "wide", scatter_dimension=0, tiled=True
        ).astype(jnp.float32),
        lax.psum_scatter(
            totals[3].astype(jnp.bfloat16), "wide", scatter_dimension=0, tiled=True
        ).astype(jnp.float32),
        lax.psum_scatter(
            totals[4].astype(jnp.bfloat16), "wide", scatter_dimension=0, tiled=True
        ).astype(jnp.float32),
    )
    summed_all = (
        lax.psum(owned_rows[0].astype(jnp.bfloat16), "narrow").astype(jnp.float32),
        lax.psum(owned_rows[1].astype(jnp.bfloat16), "narrow").astype(jnp.float32),
        lax.psum(owned_rows[2].astype(jnp.bfloat16), "narrow").astype(jnp.float32),
        lax.psum(owned_rows[3].astype(jnp.bfloat16), "narrow").astype(jnp.float32),
        lax.psum(owned_rows[4].astype(jnp.bfloat16), "narrow").astype(jnp.float32),
    )
    return (
        output,
        grad_tokens,
        summed_all[0],
        summed_all[1],
        summed_all[2],
        summed_all[3],
        summed_all[4],
    )


def solution(mesh):
    in_specs = (
        P(("wide", "narrow"), None, None),
        P(("wide", "narrow")),
        P("wide", None),
        P("wide", None),
        P("wide", None),
        P("wide", None),
        P("wide"),
        P(("wide", "narrow"), None, None),
    )
    out_specs = (
        P(("wide", "narrow"), None, None),
        P(("wide", "narrow"), None, None),
        P("wide", None),
        P("wide", None),
        P("wide", None),
        P("wide", None),
        P("wide"),
    )
    return jax.shard_map(local, mesh=mesh, in_specs=in_specs, out_specs=out_specs, check_vma=False)
```

profile of v0, /device:TPU:0, one launch (start us, length us, event | category | flops | bytes accessed | tf_op | source)
XLA Modules:
  0.0 695.1 jit_solution(4933806145959634493)
XLA Ops:
  12.9 63.8 %all-reduce = bf16[9216]{0:T(1024)(128)(2,1)S(1)} all-reduce(bf16[9216]{0:T(1024)(128)(2,1)S(1)} %dynamic-update-slice), channel_id=1, replica_groups=mesh['wide'=16,'narrow'=2] {'wide'}, use_global_device_ids=true, to_apply=%add | all-reduce | flops 9216 | bytes 36864
  77.3 4.3 fusion.45
  86.1 15.0 %while.59 = (s32[]{:T(128)}, bf16[6,512,128]{1,2,0:T(8,128)(2,1)S(1)}, f32[6,2,512]{2,1,0:T(2,128)S(1)}, bf16[6,3,512,128]{2,3,1,0:T(8,128)(2,1)S(1)}, s32[]{:T(128)}, /*index=5*/s32[]{:T(128)}, s32[]{:T(128)}, s32[]{}, s32[]{}) while((s32[]{:T(128)}, bf16[6,512,128]{1,2,0:T(8,128)(2,1)S(1)}, f32[6,2,512]{2,1,0:T(2,128)S(1)}, ...), condition=%wide.region_11.12_spmd.clone, body=%wide.region_8.11_spmd.clone.sunk | while | flops 140508672 | bytes 7899285 | solution.py:67
  106.3 19.6 %while.58 = (s32[]{:T(128)}, bf16[6,512,128]{1,2,0:T(8,128)(2,1)}, bf16[6,3,512,128]{2,3,1,0:T(8,128)(2,1)S(1)}, s32[]{:T(128)}, s32[]{:T(128)}, /*index=5*/s32[]{:T(128)}, s32[]{}, s32[]{}) while((s32[]{:T(128)}, bf16[6,512,128]{1,2,0:T(8,128)(2,1)}, bf16[6,3,512,128]{2,3,1,0:T(8,128)(2,1)S(1)}, s32[]{:T(128)}, s32[]{:T(128)}, ...), condition=%wide.region_3.4_spmd.clone, body=%wide.region_0.3_spmd.clone.sunk | while | flops 206047744 | bytes 1844873 | solution.py:67
  130.0 24.7 %all-gather.9.cloned.1.call-done = bf16[768,3072]{1,0:T(8,128)(2,1)} async-done(((bf16[48,3072]{1,0:T(8,128)(2,1)}), bf16[768,3072]{1,0:T(8,128)(2,1)}) %all-gather.9.cloned.1.call-update) | async-done | bytes 4718608 | tf_op jit(solution)/shard_map/all_gather | solution.py:212
  154.8 21.0 %multiply_convert_fusion.1 = (bf16[512,3072]{1,0:T(8,128)(2,1)}, f32[512,3072]{1,0:T(8,128)}, f32[512,3072]{1,0:T(8,128)}) fusion(f32[3072]{0:T(1024)S(1)} %slice.131, bf16[768,3072]{1,0:T(8,128)(2,1)} %all-gather.9.cloned.1.call-done, f32[512,768]{1,0:T(8,128)} %copy-done.3, f32[512]{0:T(512)S(1)} %fusion.67, f32[512]{0:T(512)S(1)} %broadcast_multiply_fusion.1, ...), kind=kOutput, calls=%fused_computation.59 | convolution fusion | flops 2521694208 | bytes 22042624 | tf_op jit(solution)/shard_map/while/body/eval_jaxpr/dot_general | solution.py:127
  175.8 33.1 %all-gather.11.cloned.1.call-done = bf16[3072,768]{1,0:T(8,128)(2,1)} async-done(((bf16[192,768]{1,0:T(8,128)(2,1)}), bf16[3072,768]{1,0:T(8,128)(2,1)}) %all-gather.11.cloned.1.call-update) | async-done | bytes 4718608 | tf_op jit(solution)/shard_map/all_gather | solution.py:213
  208.9 6.5 fusion.112
  216.9 31.5 %fusion.114 = (f32[512]{0:T(512)S(1)}, f32[512,768]{1,0:T(8,128)}) fusion(f32[768]{0:T(1024)S(1)} %get-tuple-element.323, bf16[3072,768]{1,0:T(8,128)(2,1)} %all-gather.11.cloned.1.call-done, bf16[768,3072]{1,0:T(8,128)(2,1)} %all-gather.9.cloned.1.call-done, f32[3072]{0:T(1024)S(1)} %slice.131, f32[512,768]{1,0:T(8,128)} %copy-done.9, ...), kind=kOutput, calls=%fused_computation.192 | convolution fusion | flops 4940365312 | bytes 12610560 | tf_op jit(solution)/shard_map/while/body/eval_jaxpr/dot_general | solution.py:130
  255.1 9.4 %fusion.102 = (bf16[3072]{0:T(1024)(128)(2,1)S(1)}, bf16[512,3072]{1,0:T(8,128)(2,1)}) fusion(f32[512,3072]{1,0:T(8,128)} %get-tuple-element.305, f32[512,3072]{1,0:T(8,128)} %get-tuple-element.334, f32[3072]{0:T(1024)S(1)} %slice.131, bf16[512,768]{1,0:T(8,128)(2,1)S(1)} %get-tuple-element.297, bf16[3072,768]{1,0:T(8,128)(2,1)S(1)} %copy-done.18), kind=kOutput, calls=%fused_computation.181 | convolution fusion | flops 2441081856 | bytes 21252096 | tf_op jit(solution)/shard_map/while/body/eval_jaxpr/sd,fd->sf/dot_general | solution.py:170
  264.6 5.1 multiply_reduce_fusion.1
  276.7 36.9 %while.60 = (s32[]{:T(128)}, bf16[6,3,512,128]{2,3,0,1:T(8,128)(2,1)}, bf16[6,3,512,128]{2,3,1,0:T(8,128)(2,1)S(1)}, f32[6,2,512]{2,1,0:T(2,128)}, bf16[6,512,12...) while((s32[]{:T(128)}, bf16[6,3,512,128]{2,3,0,1:T(8,128)(2,1)}, ...), condition=%wide.region_22.23_spmd.clone, body=%wide.region_20.22_spmd.clone.sunk | while | flops 341704192 | bytes 18896032 | solution.py:105
  313.6 5.6 fusion.46
  319.2 5.8 copy.52
  326.2 3.0 convolution_convert_fusion.3
  329.2 6.5 convolution_convert_fusion.1
  336.9 6.8 convolution_convert_fusion
  346.8 44.9 %reduce-scatter.13.cloned.1.call-done = bf16[48,2304]{1,0:T(8,128)(2,1)} async-done(((bf16[768,2304]{1,0:T(8,128)(2,1)}), bf16[48,2304]{1,0:T(8,128)(2,1)}) %reduce-scatter.13.cloned.1.call-update) | async-done | bytes 221200
  393.7 58.4 %reduce-scatter.7.cloned.1.call-done = bf16[48,768]{1,0:T(8,128)(2,1)} async-done(((bf16[768,768]{1,0:T(8,128)(2,1)}), bf16[48,768]{1,0:T(8,128)(2,1)}) %reduce-scatter.7.cloned.1.call-update) | async-done | bytes 73744 | tf_op jit(solution)/shard_map/reduce_scatter | solution.py:241
  452.2 78.4 %reduce-scatter.9.cloned.1.call-done = bf16[48,3072]{1,0:T(8,128)(2,1)} async-done(((bf16[768,3072]{1,0:T(8,128)(2,1)}), bf16[48,3072]{1,0:T(8,128)(2,1)}) %reduce-scatter.9.cloned.1.call-update) | async-done | bytes 294928 | tf_op jit(solution)/shard_map/reduce_scatter | solution.py:244
  530.6 79.0 %reduce-scatter.11.cloned.1.call-done = bf16[192,768]{1,0:T(8,128)(2,1)} async-done(((bf16[3072,768]{1,0:T(8,128)(2,1)}), bf16[192,768]{1,0:T(8,128)(2,1)}) %reduce-scatter.11.cloned.1.call-update) | async-done | bytes 294928 | tf_op jit(solution)/shard_map/reduce_scatter | solution.py:247
  611.3 58.0 %all-reduce.1 = bf16[9216]{0:T(1024)(128)(2,1)S(1)} all-reduce(bf16[9216]{0:T(1024)(128)(2,1)S(1)} %constant_dynamic-update-slice_fusion.2), channel_id=6, replica_groups=mesh['wide'=16,'narrow'=2] {'wide'}, use_global_device_ids=true, to_apply=%region_39.40.clone | all-reduce | flops 9216 | bytes 36864
  669.4 4.9 psum.39
  674.9 5.9 add_bitcast_fusion
  (261 shorter events, 121.5 us)
Async XLA Ops:
  7.2 70.1 %all-gather.5.cloned.1.call-start = ((), (), s32[]{:S(2)}) async-start(), calls=%async_computation.4 | async-start | bytes 3760128 | tf_op jit(solution)/shard_map/all_gather | solution.py:210
  7.9 93.3 %all-gather.7.cloned.1.call-start = ((), (), s32[]{:S(2)}) async-start(), calls=%async_computation.5 | async-start | bytes 1253376 | tf_op jit(solution)/shard_map/all_gather | solution.py:211
  8.6 146.1 %all-gather.9.cloned.1.call-start = ((), (), s32[]{:S(2)}) async-start(), calls=%async_computation.6 | async-start | bytes 5013504 | tf_op jit(solution)/shard_map/all_gather | solution.py:212
  9.4 199.5 %all-gather.11.cloned.1.call-start = ((), (), s32[]{:S(2)}) async-start(), calls=%async_computation.7 | async-start | bytes 5013504 | tf_op jit(solution)/shard_map/all_gather | solution.py:213
  10.0 381.8 %reduce-scatter.13.cloned.1.call-start = ((), (), s32[]{:S(2)}) async-start(), calls=%async_computation.11 | async-start | bytes 3760128
  101.2 2.8 copy-start.16
  101.2 4.2 copy-start.10
  216.9 33.4 %copy-start.2 = (bf16[1,512,768]{2,1,0:T(8,128)(2,1)S(1)}, bf16[1,512,768]{2,1,0:T(8,128)(2,1)}, u32[]{:S(2)}) copy-start(bf16[1,512,768]{2,1,0:T(8,128)(2,1)} %param.21) | copy-start | bytes 2359300
  216.9 33.4 %copy-start.15 = (f32[768]{0:T(1024)S(1)}, f32[768]{0:T(1024)}, u32[]{:S(2)}) copy-start(f32[768]{0:T(1024)} %get-tuple-element.319) | copy-start | bytes 9220
  248.3 4.8 copy-start.1
  248.3 4.8 copy-start.8
  248.3 4.8 copy-start.17
  248.3 6.8 copy-start.18
  253.1 11.4 %slice-start = ((s8[4718592]{0:T(1024)(128)(4,1)}), s8[4194304]{0:T(1024)(128)(4,1)S(1)}, s32[]{:S(2)}) async-start(s8[4718592]{0:T(1024)(128)(4,1)} %bitcast.216), calls=%async_computation.13 | async-start | bytes 8388608
  255.1 9.4 %copy-start.12 = (bf16[512,768]{1,0:T(8,128)(2,1)}, bf16[512,768]{1,0:T(8,128)(2,1)S(1)}, u32[]{:S(2)}) copy-start(bf16[512,768]{1,0:T(8,128)(2,1)S(1)} %get-tuple-element.297) | copy-start | bytes 2359300
  255.1 9.4 %copy-start.4 = (f32[512,768]{1,0:T(8,128)S(1)}, f32[512,768]{1,0:T(8,128)}, u32[]{:S(2)}) copy-start(f32[512,768]{1,0:T(8,128)} %copy-done.3) | copy-start | bytes 4718596
  255.1 9.4 %slice-start.1 = ((s8[4718592]{0:T(1024)(128)(4,1)}), s8[524288]{0:T(1024)(128)(4,1)S(1)}, s32[]{:S(2)}) async-start(s8[4718592]{0:T(1024)(128)(4,1)} %bitcast.216), calls=%async_computation.14 | async-start | bytes 1048576
  269.7 3.0 copy-start.19
  325.1 4.1 copy-start.5
  325.1 127.1 %reduce-scatter.7.cloned.1.call-start = ((), (), s32[]{:S(2)}) async-start(), calls=%async_computation.8 | async-start | bytes 1253376 | tf_op jit(solution)/shard_map/reduce_scatter | solution.py:241
  329.2 201.5 %reduce-scatter.9.cloned.1.call-start = ((), (), s32[]{:S(2)}) async-start(), calls=%async_computation.9 | async-start | bytes 5013504 | tf_op jit(solution)/shard_map/reduce_scatter | solution.py:244
  335.8 273.9 %reduce-scatter.11.cloned.1.call-start = ((), (), s32[]{:S(2)}) async-start(), calls=%async_computation.10 | async-start | bytes 5013504 | tf_op jit(solution)/shard_map/reduce_scatter | solution.py:247
  343.8 331.2 %copy-start.7 = (f32[512,768]{1,0:T(8,128)S(1)}, f32[512,768]{1,0:T(8,128)}, u32[]{:S(2)}) copy-start(f32[512,768]{1,0:T(8,128)} %copy-done.6) | copy-start | bytes 4718596
  343.8 337.1 %all-reduce.5.cloned.1.call-start = ((), (), s32[]{:S(2)}) async-start(), calls=%async_computation.12 | async-start | bytes 2506752 | tf_op jit(solution)/shard_map/psum | solution.py:255
  (7 other events, 7.9 us)
Sparse Core Ops, SparseCore 0:
  10.3 50.1 all-gather.4
  62.7 37.4 all-gather.6
  102.5 52.2 all-gather.8
  156.9 51.9 all-gather.10
  325.2 66.5 reduce-scatter.12
  395.2 56.9 reduce-scatter.6
  456.0 74.5 reduce-scatter.8
  535.0 74.6 reduce-scatter.10
  612.7 44.0 all-reduce.4
where the time goes:
time: 703 us; the launch traced here: 695 us
  waiting for transfers between devices  321 us (46%)
  matrix products  146 us (21%)
  blocking collectives  127 us (18%)
  local copies, waits for them, and re-layouts  43.9 us (6%)
  other arithmetic  39.4 us (6%)
  between operations  16.1 us (2%)
    unnamed x2, blocking collectives  122 us
    reduce_scatter x1, waiting for transfers between devices, local(): lax.psum_scatter(totals[3].astype(jnp.bfloat16), 'wide', scatter_dimensio...  79 us
    reduce_scatter x1, waiting for transfers between devices, local(): lax.psum_scatter(totals[2].astype(jnp.bfloat16), 'wide', scatter_dimensio...  78.4 us
    reduce_scatter x1, waiting for transfers between devices, local(): lax.psum_scatter(totals[1].astype(jnp.bfloat16), 'wide', scatter_dimensio...  58.4 us
    unnamed x10, waiting for transfers between devices  47.6 us
    dot_general x2, matrix products, layer_forward(): jnp.dot(activated, w_down, preferred_element_type=jnp.float32) + params[5]  37.9 us
    all_gather x1, waiting for transfers between devices, local(): lax.all_gather(w_down, 'wide', axis=0, tiled=True)  33.1 us
    all_gather x1, waiting for transfers between devices, local(): lax.all_gather(w_in, 'wide', axis=0, tiled=True)  24.7 us
  transfers between devices with their start and end apart: 9, of which 6 were waited for; matrix products, arithmetic and copies ran while one was open for 15% of the time, Pallas kernels for 0%

commit v1 on v0

--- a/solution.py
+++ b/solution.py
@@ -1,9 +1,877 @@
+import functools
+
 import jax
 import jax.numpy as jnp
+import numpy as np
 from jax import lax
+from jax.experimental import pallas as pl
+from jax.experimental.pallas import tpu as pltpu
 from jax.sharding import PartitionSpec as P
 
 HEADS = 12
+MESH = pl.DeviceIdType.MESH
+BF = jnp.bfloat16
+F32 = jnp.float32
+NT = (((1,), (1,)), ((), ()))
+TN = (((0,), (0,)), ((), ()))
+ZH, ZL, YS, CS = 2, 2, 2, 2
+ZS = ZH * ZL
+QKV, OUT, IN, DOWN, CHUNKS = 0, 3, 4, 8, 12
+SQRT_HALF = 0.7071067811865476
+INV_SQRT_TAU = 0.3989422804014327
+
+
+def dot(left, right, dims=None):
+    if dims is None:
+        return jnp.dot(left, right, preferred_element_type=F32)
+    return lax.dot_general(left, right, dims, preferred_element_type=F32)
+
+
+def loop(count, body):
+    def step(index, carry):
+        body(index)
+        return carry
+
+    lax.fori_loop(0, count, step, 0)
+
+
+def span(index, size):
+    return pl.ds(pl.multiple_of(index * size, size), size)
+
+
+def layer_kernel(
+    x_hbm, len_ref, wqkv_hbm, wout_hbm, win_hbm, wdown_hbm, vec_hbm, cot_hbm,
+    out_hbm, gtok_hbm, gqkv_hbm, gout_hbm, gin_hbm, gdown_hbm, gvec_hbm,
+    wa, wd, vb, gd, go, gv, rcore, rya, rxb, rza, ryb, rzb, rxa, rfb, rv_core, rv_y, rv_z, rv_x, fin, fv,
+    x, cot, qkv, vt, pt, ct, n1, y1b, y1t, act, dact, h2, dfb, dcx, rs1, prm, vg,
+    s_load, s_vload, s_io, s_store,
+    gsz, grz, gsy, gry, gsx1, grx1, gsx2, grx2, gsc, grc, vsz, vrz, vsy, vry, vsc, vrc,
+    rsc, rrc, rsya, rrya, rsxb, rrxb, rsza, rrza, rsyb, rryb, rszb, rrzb, rsxa, rrxa, rsfb, rrfb,
+    wsc, wrc, wsy, wry, wsz, wrz, wsx, wrx,
+):
+    seq, model = x.shape
+    rows = wa.shape[-2]
+    hidden = act.shape[1]
+    pair = 2 * (model // HEADS)
+    head = model // HEADS
+    group = model // 3
+    half = model // 2
+    wide = lax.axis_index("wide")
+    px = lax.axis_index("narrow")
+    c = lax.rem(wide, CS)
+    y = lax.rem(wide // CS, YS)
+    z = wide // (CS * YS)
+    zl = lax.rem(z, ZL)
+    zh = z // ZL
+
+    def device(zz, yy, cc, xx):
+        return ((zz * YS + yy) * CS + cc, xx)
+
+    sibling = device(z, y, 1 - c, px)
+    across_y = device(z, 1 - y, c, px)
+    across_x = device(z, y, c, 1 - px)
+
+    def ahead(dz):
+        return lax.rem(z + dz, ZS)
+
+    def behind(dz):
+        return lax.rem(z + ZS - dz, ZS)
+
+    def remote(src, dst, send, recv, where):
+        return pltpu.make_async_remote_copy(
+            src_ref=src, dst_ref=dst, send_sem=send, recv_sem=recv, device_id=where, device_id_type=MESH
+        )
+
+    ALL = slice(None)
+
+    def wpiece(k, zz, yy, cc, r=ALL):
+        zi = (ALL, ALL) if zz is None else (zz // ZL, lax.rem(zz, ZL))
+        if k < DOWN:
+            return wa.at[(k, *zi, yy, cc, r)]
+        return wd.at[(*zi, yy, cc, k - DOWN, r)]
+
+    loads = []
+
+    def load(src, dst, sem):
+        cp = pltpu.make_async_copy(src, dst, sem)
+        cp.start()
+        return cp
+
+    own_loads = [[] for _ in range(CHUNKS)]
+    load_vec = load(vec_hbm, vb.at[zh, zl, y, c], s_vload)
+    load_x = load(x_hbm.at[0], x, s_io.at[0])
+    for k in range(CHUNKS):
+        if k < OUT:
+            for part in range(3):
+                own_loads[k].append(
+                    load(
+                        wqkv_hbm.at[:, pl.ds(part * model + k * group, group)],
+                        wa.at[k, zh, zl, y, c, :, pl.ds(part * group, group)],
+                        s_load.at[k, part],
+                    )
+                )
+        elif k < IN:
+            own_loads[k].append(load(wout_hbm, wa.at[k, zh, zl, y, c], s_load.at[k, 0]))
+        elif k < DOWN:
+            own_loads[k].append(
+                load(win_hbm.at[:, pl.ds((k - IN) * model, model)], wa.at[k, zh, zl, y, c], s_load.at[k, 0])
+            )
+        else:
+            own_loads[k].append(
+                load(wdown_hbm.at[pl.ds((k - DOWN) * rows, rows)], wd.at[zh, zl, y, c, k - DOWN], s_load.at[k, 0])
+            )
+    load_cot = load(cot_hbm.at[0], cot, s_io.at[1])
+
+    barrier = pltpu.get_barrier_semaphore()
+    for where in (sibling, across_y, across_x, *(device(ahead(dz), y, c, px) for dz in (1, 2, 3))):
+        pl.semaphore_signal(barrier, inc=1, device_id=where, device_id_type=MESH)
+    pl.semaphore_wait(barrier, 6)
+
+    third = rows // 3
+    kept = pl.ds(pl.multiple_of(px * third, third), 2 * third)
+    given = pl.ds(pl.multiple_of(px * 2 * third, third), third)
+    taken = pl.ds(pl.multiple_of((1 - px) * 2 * third, third), third)
+
+    def g_z(k, dz, source):
+        piece = wpiece(k, source, y, c, kept)
+        return remote(piece, piece, gsz.at[k, dz - 1], grz.at[k, dz - 1], device(ahead(dz), y, c, px))
+
+    def g_y(k, column):
+        piece = wpiece(k, None, column, c, kept)
+        return remote(piece, piece, gsy.at[k], gry.at[k], across_y)
+
+    def g_x1(k, dz, r):
+        piece = wpiece(k, behind(dz), y, c, r)
+        return remote(piece, piece, gsx1.at[k, dz - 1], grx1.at[k, dz - 1], across_x)
+
+    def g_x2(k, r):
+        piece = wpiece(k, None, 1 - y, c, r)
+        return remote(piece, piece, gsx2.at[k], grx2.at[k], across_x)
+
+    def g_core(k, core):
+        piece = wpiece(k, None, ALL, core)
+        return remote(piece, piece, gsc.at[k], grc.at[k], sibling)
+
+    def v_z(dz, source):
+        piece = vb.at[source // ZL, lax.rem(source, ZL), y, c]
+        return remote(piece, piece, vsz.at[dz - 1], vrz.at[dz - 1], device(ahead(dz), y, c, px))
+
+    def v_y(column):
+        piece = vb.at[:, :, column, c]
+        return remote(piece, piece, vsy, vry, across_y)
+
+    def v_core(core):
+        piece = vb.at[:, :, :, core]
+        return remote(piece, piece, vsc, vrc, sibling)
+
+    def e1(k):
+        if not 0 <= k < CHUNKS:
+            return
+        for cp in own_loads[k]:
+            cp.wait()
+        if k == 0:
+            load_vec.wait()
+            for dz in (1, 2, 3):
+                v_z(dz, z).start()
+        for dz in (1, 2, 3):
+            g_z(k, dz, z).start()
+
+    def e2(k):
+        if not 0 <= k < CHUNKS:
+            return
+        if k == 0:
+            for dz in (1, 2, 3):
+                v_z(dz, behind(dz)).wait_recv()
+            v_y(y).start()
+        for dz in (1, 2, 3):
+            g_z(k, dz, behind(dz)).wait_recv()
+        g_y(k, y).start()
+        for dz in (1, 2, 3):
+            g_x1(k, dz, given).start()
+
+    def e3(k):
+        if not 0 <= k < CHUNKS:
+            return
+        if k == 0:
+            v_y(1 - y).wait_recv()
+            v_core(c).start()
+        g_y(k, 1 - y).wait_recv()
+        g_x2(k, given).start()
+
+    def e4(k):
+        if not 0 <= k < CHUNKS:
+            return
+        for dz in (1, 2, 3):
+            g_x1(k, dz, taken).wait_recv()
+        g_x2(k, taken).wait_recv()
+        g_core(k, c).start()
+
+    def e5(k):
+        if not 0 <= k < CHUNKS:
+            return
+        if k == 0:
+            v_core(1 - c).wait_recv()
+        g_core(k, 1 - c).wait_recv()
+
+    def sent(k):
+        for dz in (1, 2, 3):
+            g_z(k, dz, z).wait_send()
+            g_x1(k, dz, given).wait_send()
+        g_y(k, y).wait_send()
+        g_x2(k, given).wait_send()
+        g_core(k, c).wait_send()
+
+    def vec_sent():
+        for dz in (1, 2, 3):
+            v_z(dz, z).wait_send()
+        v_y(y).wait_send()
+        v_core(c).wait_send()
+
+    def place_matrix(k, lanes):
+        i = lax.broadcasted_iota(jnp.int32, (lanes, model), 0)
+        j = lax.broadcasted_iota(jnp.int32, (lanes, model), 1)
+        quarter = model // 4
+        return jnp.where((i < quarter) & (j == i + k * quarter), 1.0, 0.0).astype(BF)
+
+    def pick_matrix(k, count, total, slot):
+        b = lax.broadcasted_iota(jnp.int32, (count, total), 0)
+        r = lax.broadcasted_iota(jnp.int32, (count, total), 1)
+        segment = 4 * b + k
+        return jnp.where((r == slot * (segment // 3) + lax.rem(segment, 3)) & (b < 12), 1.0, 0.0).astype(BF)
+
+    def spread_params():
+        lanes = vb.shape[-1]
+        segments = vb[...].reshape(-1, lanes)
+        total = None
+        for k in range(4):
+            picked = dot(pick_matrix(k, 16, segments.shape[0], vb.shape[-2]), segments).astype(BF)
+            part = dot(picked, place_matrix(k, lanes))
+            total = part if total is None else total + part
+        prm[...] = total
+
+    def gather_grads():
+        lanes = gv.shape[-1]
+        low = vg[...].astype(BF)
+        total = None
+        for k in range(4):
+            cut = dot(low, place_matrix(k, lanes), NT).astype(BF)
+            part = dot(pick_matrix(k, 16, 16 * gv.shape[-2], gv.shape[-2]), cut, TN)
+            total = part if total is None else total + part
+        gv[...] = total.astype(BF).reshape(gv.shape)
+
+    def weight(k, cols=ALL):
+        block = wa[k, :, :, :, :, :, cols]
+        return block.reshape(-1, block.shape[-1])
+
+    def project(g):
+        grouped = span(g, group)
+        joined = dot(x[...], weight(g))
+        q = (joined[:, :group] + prm[0:1, grouped]).astype(BF)
+        qkv[g, :, 0:group] = q * jnp.asarray(head**-0.5, BF)
+        qkv[g, :, group : 2 * group] = joined[:, group : 2 * group].astype(BF)
+        v = (joined[:, 2 * group :] + prm[1:2, grouped]).astype(BF)
+        qkv[g, :, 2 * group :] = v
+        vt[grouped, :] = v.T
+
+    def attend(g):
+        length = len_ref[0]
+
+        def one(h):
+            cols = span(h // 2, pair)
+            keys = pl.ds(pl.multiple_of(group + (h // 2) * pair, pair), pair)
+            lane = lax.broadcasted_iota(jnp.int32, (seq, pair), 1) // head
+            masked = jnp.where(lane == lax.rem(h, 2), qkv[g, :, keys], jnp.zeros((), BF))
+            scores = dot(masked, qkv[g, :, cols], NT)
+            key = lax.broadcasted_iota(jnp.int32, scores.shape, 0)
+            scores = jnp.where(key < length, scores, -1000000000.0)
+            raised = jnp.exp(scores - jnp.max(scores, axis=0, keepdims=True))
+            probs = (raised * (1.0 / jnp.sum(raised, axis=0, keepdims=True))).astype(BF)
+            pt[g, h] = probs
+            mine = pl.ds(pl.multiple_of(g * group + h * head, head), head)
+            ct[mine, :] = dot(vt[mine, :], probs).astype(BF)
+
+        loop(group // head, one)
+
+    def out_proj():
+        context = ct[...].T
+        bo, g1, c1 = prm[2:3, :], prm[3:4, :], prm[4:5, :]
+        w = weight(OUT)
+
+        def tile(i):
+            r = span(i, 128)
+            h1 = x[r, :].astype(F32) + (h2[r, :] + bo)
+            centred = h1 - jnp.mean(h1, -1, keepdims=True)
+            inverse = lax.rsqrt(jnp.mean(centred * centred, -1, keepdims=True) + 1e-06)
+            normed = centred * inverse
+            n1[r, :] = normed
+            rs1[r, :] = inverse
+            y1b[r, :] = (normed * g1 + c1).astype(BF)
+
+        h2[...] = dot(context, w)
+        loop(seq // 128, tile)
+
+    def feed_up(j):
+        def tile(i):
+            cols = span(i, 256)
+            wide_cols = pl.ds(pl.multiple_of(j * model + i * 256, 256), 256)
+            u = dot(y1b[...], weight(IN + j, cols)) + prm[8 + j : 9 + j, cols]
+            phi = 0.5 * (1.0 + lax.erf(u * SQRT_HALF))
+            act[:, wide_cols] = (u * phi).astype(BF)
+            dact[:, wide_cols] = (phi + u * (jnp.exp(-0.5 * u * u) * INV_SQRT_TAU)).astype(BF)
+
+        loop(model // 256, tile)
+
+    def feed_down():
+        def tile(i):
+            cols = span(i, 256)
+            w = wd[:, :, :, :, :, :, cols].reshape(hidden, 256)
+            y1 = n1[:, cols] * prm[3:4, cols] + prm[4:5, cols]
+            h2[:, cols] = y1 + (dot(act[...], w) + prm[5:6, cols])
+
+        loop(model // 256, tile)
+
+    def vsum(row, value):
+        vg[row : row + 1, :] += jnp.sum(value, axis=0, keepdims=True)
+
+    def norm_back(dn, n, inverse):
+        return (dn - jnp.mean(dn, -1, keepdims=True) - n * jnp.mean(dn * n, -1, keepdims=True)) * inverse
+
+    def norm_two():
+        g2, c2 = prm[6:7, :], prm[7:8, :]
+
+        def tile(i):
+            r = span(i, 128)
+            h = h2[r, :]
+            centred = h - jnp.mean(h, -1, keepdims=True)
+            inverse = lax.rsqrt(jnp.mean(centred * centred, -1, keepdims=True) + 1e-06)
+            n = centred * inverse
+            dcx[r, :] = (n * g2 + c2).astype(BF)
+            dy = cot[r, :].astype(F32)
+            vsum(6, dy * n)
+            vsum(7, dy)
+            dh = norm_back(dy * g2, n, inverse)
+            h2[r, :] = dh
+            low = dh.astype(BF)
+            dfb[r, :] = low
+            vsum(5, low.astype(F32))
+
+        loop(seq // 128, tile)
+
+    def grad_down():
+        def tile(i):
+            cols = span(i, 2 * 4 * rows)
+            g = dot(act[:, cols], dfb[...], TN).astype(BF).reshape(CS, 4, rows, model)
+            zz = i // YS
+            gd[zz // ZL, lax.rem(zz, ZL), lax.rem(i, YS)] = g
+
+        loop(ZS * YS, tile)
+
+    def grad_act(j):
+        def tile(t):
+            i = 2 * j + t
+            cols = span(i, 2 * 4 * rows)
+            zz = i // YS
+            w = wd[zz // ZL, lax.rem(zz, ZL), lax.rem(i, YS)].reshape(2 * 4 * rows, model)
+            du = (dot(dfb[...], w, NT) * dact[:, cols].astype(F32)).astype(BF)
+            dact[:, cols] = du
+            total = jnp.sum(du.astype(F32), axis=0, keepdims=True)
+            if t == 0:
+                vg[8 + j : 9 + j, 0:half] = total
+            else:
+                vg[8 + j : 9 + j, half:] = total
+
+        tile(0)
+        tile(1)
+
+    def grad_in(j):
+        if j == 0:
+            y1t[...] = y1b[...].T
+
+        def tile(i):
+            cols = span(i, 256)
+            wide_cols = pl.ds(pl.multiple_of(j * model + i * 256, 256), 256)
+            g = dot(y1t[...], dact[:, wide_cols]).astype(BF)
+            wd[:, :, :, :, j, :, cols] = g.reshape(ZH, ZL, YS, CS, rows, 256)
+
+        loop(model // 256, tile)
+
+    def grad_normed(j):
+        def tile(i):
+            cols = span(i, half)
+            w = wa[IN + j, i].reshape(half, model)
+            h2[:, cols] += dot(dact[:, j * model : (j + 1) * model], w, NT)
+
+        loop(2, tile)
+
+    def norm_one_back():
+        g1 = prm[3:4, :]
+
+        def tile(i):
+            r = span(i, 128)
+            dy, n = h2[r, :], n1[r, :]
+            vsum(3, dy * n)
+            vsum(4, dy)
+            dh = norm_back(dy * g1, n, rs1[r, :])
+            h2[r, :] = dh
+            low = dh.astype(BF)
+            dfb[r, :] = low
+            vsum(2, low.astype(F32))
+
+        loop(seq // 128, tile)
+
+    def grad_out():
+        g = dot(ct[...], dfb[...]).astype(BF)
+        go[0] = g.reshape(ZH, ZL, YS, CS, rows, model)
+
+    def grad_context():
+        vt[...] = x[...].T
+        dcx[...] = dot(dfb[...], weight(OUT), NT).astype(BF)
+
+    def attend_back(g):
+        def one(j):
+            cols = span(j, pair)
+            keys = pl.ds(pl.multiple_of(group + j * pair, pair), pair)
+            vals = pl.ds(pl.multiple_of(2 * group + j * pair, pair), pair)
+            wide_cols = pl.ds(pl.multiple_of(g * group + j * pair, pair), pair)
+            lane = lax.broadcasted_iota(jnp.int32, (seq, pair), 1) // head
+            dc = dcx[:, wide_cols]
+            q, k, v = qkv[g, :, cols], qkv[g, :, keys], qkv[g, :, vals]
+            kt = k.T
+            dk, dv, dq = [], [], []
+            for e in range(2):
+                probs = pt[g, 2 * j + e]
+                dv.append(dot(probs, dc))
+                dp = dot(jnp.where(lane == e, v, jnp.zeros((), BF)), dc, NT)
+                p32 = probs.astype(F32)
+                t = p32 * dp
+                ds = (t - p32 * jnp.sum(t, axis=0, keepdims=True)).astype(BF)
+                dk.append(dot(ds, q))
+                dq.append((dot(kt[e * head : (e + 1) * head, :], ds) * head**-0.5).astype(BF))
+            qkv[g, :, cols] = jnp.concatenate(dq, axis=0).T
+            qkv[g, :, keys] = jnp.where(lane == 0, dk[0], dk[1]).astype(BF)
+            qkv[g, :, vals] = jnp.where(lane == 0, dv[0], dv[1]).astype(BF)
+
+        loop(group // pair, one)
+        grouped = span(g, group)
+        vg[0:1, grouped] = jnp.sum(qkv[g, :, 0:group].astype(F32), axis=0, keepdims=True)
+        vg[1:2, grouped] = jnp.sum(qkv[g, :, 2 * group :].astype(F32), axis=0, keepdims=True)
+
+    def grad_qkv(g):
+        r = dot(vt[...], qkv[g]).astype(BF)
+        wa[IN + g] = r.reshape(ZH, ZL, YS, CS, rows, model)
+
+    def grad_x():
+        total = h2[...]
+        for g in range(3):
+            total = total + dot(qkv[g], weight(g), NT)
+        n1[...] = total
+
+    left, right = pl.ds(0, half), pl.ds(half, half)
+
+    def gpiece(k, zi, yy, cc, cols=ALL):
+        if k < 4:
+            return gd.at[(*zi, yy, cc, k, ALL, cols)]
+        if k < 8:
+            return wd.at[(*zi, yy, cc, k - 4, ALL, cols)]
+        if k < 9:
+            return go.at[(0, *zi, yy, cc, ALL, cols)]
+        return wa.at[(IN + k - 9, *zi, yy, cc, ALL, cols)]
+
+    every = (ALL, ALL)
+    mine = (zh, zl)
+
+    def at_z(zz):
+        return (zz // ZL, lax.rem(zz, ZL))
+
+    def r_core(k):
+        return remote(gpiece(k, every, ALL, 1 - c), rcore.at[k], rsc.at[k], rrc.at[k], sibling)
+
+    def r_ya(k):
+        return remote(gpiece(k, every, 1 - y, c, left), rya.at[k], rsya.at[k], rrya.at[k], across_y)
+
+    def r_xb(k):
+        return remote(gpiece(k, (ALL, 1 - px), ALL, c, right), rxb.at[k], rsxb.at[k], rrxb.at[k], across_x)
+
+    def r_za(k, dz):
+        piece = gpiece(k, at_z(ahead(dz)), y, c, left)
+        return remote(piece, rza.at[k, dz - 1], rsza.at[k, dz - 1], rrza.at[k, dz - 1], device(ahead(dz), y, c, px))
+
+    def r_yb(k):
+        return remote(gpiece(k, (ALL, px), 1 - y, c, right), ryb.at[k], rsyb.at[k], rryb.at[k], across_y)
+
+    def r_xa(k):
+        return remote(gpiece(k, mine, y, c, left), rxa.at[k], rsxa.at[k], rrxa.at[k], across_x)
+
+    def r_zb(k, dz):
+        piece = gpiece(k, at_z(ahead(dz)), y, c, right)
+        return remote(piece, rzb.at[k, dz - 1], rszb.at[k, dz - 1], rrzb.at[k, dz - 1], device(ahead(dz), y, c, px))
+
+    def r_fb(k):
+        return remote(gpiece(k, mine, y, c, right), rfb.at[k], rsfb.at[k], rrfb.at[k], across_x)
+
+    same = zl == px
+
+    def to_parity(dz, act_on):
+        if dz == 2:
+            pl.when(same)(act_on)
+        else:
+            pl.when(jnp.logical_not(same))(act_on)
+
+    def add_into(ref, *others):
+        total = ref[...].astype(F32)
+        for other in others:
+            total = total + other[...].astype(F32)
+        ref[...] = total.astype(BF)
+
+    def n_chunk(k):
+        return 0 <= k < CHUNKS
+
+    def r0(k):
+        if n_chunk(k):
+            r_core(k).start()
+        if k == CHUNKS - 1:
+            remote(gv.at[:, :, :, 1 - c], rv_core, wsc, wrc, sibling).start()
+
+    def r1(k):
+        if not n_chunk(k):
+            return
+        r_core(k).wait_recv()
+
+        def add(i):
+            piece = gpiece(k, at_z(i), ALL, c)
+            add_into(piece, rcore.at[(k, *at_z(i))])
+
+        loop(ZS, add)
+        r_ya(k).start()
+        r_xb(k).start()
+        if k == CHUNKS - 1:
+            remote(gv.at[:, :, :, 1 - c], rv_core, wsc, wrc, sibling).wait_recv()
+            add_into(gv.at[:, :, :, c], rv_core)
+            remote(gv.at[:, :, 1 - y, c], rv_y, wsy, wry, across_y).start()
+
+    def v_rz(dz):
+        return remote(
+            gv.at[(*at_z(ahead(dz)), y, c)], rv_z.at[dz - 1], wsz.at[dz - 1], wrz.at[dz - 1],
+            device(ahead(dz), y, c, px),
+        )
+
+    def v_rx():
+        return remote(gv.at[(*mine, y, c)], rv_x, wsx, wrx, across_x)
+
+    def r2(k):
+        if not n_chunk(k):
+            return
+        r_ya(k).wait_recv()
+        add_into(gpiece(k, every, y, c, left), rya.at[k])
+        for dz in (1, 2, 3):
+            r_za(k, dz).start()
+        r_xb(k).wait_recv()
+        add_into(gpiece(k, (ALL, px), ALL, c, right), rxb.at[k])
+        r_yb(k).start()
+        if k == CHUNKS - 1:
+            remote(gv.at[:, :, 1 - y, c], rv_y, wsy, wry, across_y).wait_recv()
+            add_into(gv.at[:, :, y, c], rv_y)
+            for dz in (1, 2, 3):
+                v_rz(dz).start()
+
+    def r3(k):
+        if not n_chunk(k):
+            return
+        r_yb(k).wait_recv()
+        add_into(gpiece(k, (ALL, px), y, c, right), ryb.at[k])
+        for dz in (1, 2, 3):
+            to_parity(dz, lambda dz=dz: r_zb(k, dz).start())
+        for dz in (1, 2, 3):
+            r_za(k, dz).wait_recv()
+        add_into(gpiece(k, mine, y, c, left), rza.at[k, 0], rza.at[k, 1], rza.at[k, 2])
+        r_xa(k).start()
+        if k == CHUNKS - 1:
+            for dz in (1, 2, 3):
+                v_rz(dz).wait_recv()
+            add_into(gv.at[(*mine, y, c)], rv_z.at[0], rv_z.at[1], rv_z.at[2])
+            v_rx().start()
+
+    def r4(k):
+        if not n_chunk(k):
+            return
+
+        @pl.when(same)
+        def _():
+            for dz in (1, 2, 3):
+                r_zb(k, dz).wait_recv()
+            add_into(gpiece(k, mine, y, c, right), rzb.at[k, 0], rzb.at[k, 1], rzb.at[k, 2])
+            r_fb(k).start()
+            fin[k, :, right] = gpiece(k, mine, y, c, right)[...].astype(F32)
+
+        r_xa(k).wait_recv()
+        fin[k, :, left] = gpiece(k, mine, y, c, left)[...].astype(F32) + rxa[k].astype(F32)
+        if k == CHUNKS - 1:
+            v_rx().wait_recv()
+            fv[...] = gv[(*mine, y, c)].astype(F32) + rv_x[...].astype(F32)
+
+    stores = []
+
+    def store(src, dst):
+        cp = pltpu.make_async_copy(src, dst, s_store.at[len(stores)])
+        cp.start()
+        stores.append(cp)
+
+    def r5(k):
+        if not n_chunk(k):
+            return
+
+        @pl.when(jnp.logical_not(same))
+        def _():
+            r_fb(k).wait_recv()
+            fin[k, :, right] = rfb[k].astype(F32)
+
+        if k < 4:
+            store(fin.at[k], gdown_hbm.at[pl.ds(k * rows, rows)])
+        elif k < 8:
+            store(fin.at[k], gin_hbm.at[:, pl.ds((k - 4) * model, model)])
+        elif k < 9:
+            store(fin.at[k], gout_hbm)
+        else:
+            for part in range(3):
+                store(
+                    fin.at[k, :, pl.ds(part * group, group)],
+                    gqkv_hbm.at[:, pl.ds(part * model + (k - 9) * group, group)],
+                )
+
+    def sums_sent(k):
+        r_core(k).wait_send()
+        r_ya(k).wait_send()
+        r_xb(k).wait_send()
+        r_yb(k).wait_send()
+        r_xa(k).wait_send()
+        for dz in (1, 2, 3):
+            r_za(k, dz).wait_send()
+            to_parity(dz, lambda dz=dz: r_zb(k, dz).wait_send())
+        pl.when(same)(lambda: r_fb(k).wait_send())
+
+    vg[...] = jnp.zeros_like(vg)
+    e1(0)
+    e1(1)
+    load_x.wait()
+
+    def forward(k):
+        if k < 0:
+            return
+        if k < OUT:
+            if k == 0:
+                spread_params()
+            project(k)
+            attend(k)
+        elif k < IN:
+            out_proj()
+        elif k < DOWN:
+            feed_up(k - IN)
+
+    for t in range(1, CHUNKS + 4):
+        e5(t - 4)
+        e4(t - 3)
+        e3(t - 2)
+        e2(t - 1)
+        e1(t + 1)
+        forward(t - 4)
+    load_cot.wait()
+    feed_down()
+    norm_two()
+    store(dcx, out_hbm.at[0])
+    grad_down()
+    for k in range(4):
+        r0(k)
+    r1(0)
+    grad_act(0)
+    grad_act(1)
+    r1(1)
+    r2(0)
+    grad_act(2)
+    grad_act(3)
+    r1(2)
+    r2(1)
+    r3(0)
+    for k in range(DOWN, CHUNKS):
+        sent(k)
+    grad_in(0)
+    r0(4)
+    grad_in(1)
+    r0(5)
+    r1(3)
+    r2(2)
+    r3(1)
+    r4(0)
+    grad_in(2)
+    r0(6)
+    grad_in(3)
+    r0(7)
+    r1(4)
+    r2(3)
+    r3(2)
+    r4(1)
+    r5(0)
+    grad_normed(0)
+    grad_normed(1)
+    r1(5)
+    r2(4)
+    r3(3)
+    r4(2)
+    r5(1)
+    grad_normed(2)
+    grad_normed(3)
+    norm_one_back()
+    r1(6)
+    r2(5)
+    r3(4)
+    r4(3)
+    r5(2)
+    stores[0].wait()
+    grad_out()
+    r0(8)
+    grad_context()
+    for k in range(IN, DOWN):
+        sent(k)
+    r1(7)
+    r2(6)
+    r3(5)
+    r4(4)
+    r5(3)
+    attend_back(0)
+    grad_qkv(0)
+    r0(9)
+    r1(8)
+    r2(7)
+    r3(6)
+    r4(5)
+    r5(4)
+    attend_back(1)
+    grad_qkv(1)
+    r0(10)
+    r1(9)
+    r2(8)
+    r3(7)
+    r4(6)
+    r5(5)
+    attend_back(2)
+    grad_qkv(2)
+    gather_grads()
+    r0(11)
+    r1(10)
+    r2(9)
+    r3(8)
+    r4(7)
+    r5(6)
+    r1(11)
+    grad_x()
+    store(n1, gtok_hbm.at[0])
+    r2(10)
+    r3(9)
+    r4(8)
+    r5(7)
+    r2(11)
+    r3(10)
+    r4(9)
+    r5(8)
+    r3(11)
+    r4(10)
+    r5(9)
+    r4(11)
+    store(fv, gvec_hbm)
+    r5(10)
+    r5(11)
+    for k in range(IN):
+        sent(k)
+    vec_sent()
+    for k in range(CHUNKS):
+        sums_sent(k)
+    remote(gv.at[:, :, :, 1 - c], rv_core, wsc, wrc, sibling).wait_send()
+    remote(gv.at[:, :, 1 - y, c], rv_y, wsy, wry, across_y).wait_send()
+    for dz in (1, 2, 3):
+        v_rz(dz).wait_send()
+    v_rx().wait_send()
+    for cp in stores[1:]:
+        cp.wait()
+
+
+def fused_layer(tokens, lengths, w_qkv, w_out, w_in, w_down, norms_biases, cotangent):
+    seq, model = tokens.shape[1:]
+    rows = w_qkv.shape[0]
+    hidden = w_in.shape[1]
+    half = model // 2
+    group = model // 3
+    segments = jnp.pad(norms_biases.reshape(3, -1), ((0, 13), (0, 256 - norms_biases.shape[0] // 3)))
+    vm, dma = pltpu.VMEM, pltpu.SemaphoreType.DMA
+    grid = (ZH, ZL, YS, CS)
+    n = CHUNKS
+    scratch = [
+        vm((DOWN, *grid, rows, model), BF),
+        vm((*grid, 4, rows, model), BF),
+        vm((*grid, 16, 256), BF),
+        vm((*grid, 4, rows, model), BF),
+        vm((1, *grid, rows, model), BF),
+        vm((*grid, 16, 256), BF),
+        vm((n, ZH, ZL, YS, rows, model), BF),
+        vm((n, ZH, ZL, rows, half), BF),
+        vm((n, ZH, YS, rows, half), BF),
+        vm((n, 3, rows, half), BF),
+        vm((n, ZH, rows, half), BF),
+        vm((n, 3, rows, half), BF),
+        vm((n, rows, half), BF),
+        vm((n, rows, half), BF),
+        vm((ZH, ZL, YS, 16, 256), BF),
+        vm((ZH, ZL, 16, 256), BF),
+        vm((3, 16, 256), BF),
+        vm((16, 256), BF),
+        vm((n, rows, model), F32),
+        vm((16, 256), F32),
+        vm((seq, model), BF),
+        vm((seq, model), BF),
+        vm((3, seq, model), BF),
+        vm((model, seq), BF),
+        vm((3, group // (model // HEADS), seq, seq), BF),
+        vm((model, seq), BF),
+        vm((seq, model), F32),
+        vm((seq, model), BF),
+        vm((model, seq), BF),
+        vm((seq, hidden), BF),
+        vm((seq, hidden), BF),
+        vm((seq, model), F32),
+        vm((seq, model), BF),
+        vm((seq, model), BF),
+        vm((seq, 1), F32),
+        vm((16, model), F32),
+        vm((16, model), F32),
+        dma((n, 3)), dma, dma((2,)), dma((21,)),
+        dma((n, 3)), dma((n, 3)), dma((n,)), dma((n,)), dma((n, 3)), dma((n, 3)),
+        dma((n,)), dma((n,)), dma((n,)), dma((n,)),
+        dma((3,)), dma((3,)), dma, dma, dma, dma,
+        dma((n,)), dma((n,)), dma((n,)), dma((n,)), dma((n,)), dma((n,)), dma((n, 3)), dma((n, 3)),
+        dma((n,)), dma((n,)), dma((n, 3)), dma((n, 3)), dma((n,)), dma((n,)), dma((n,)), dma((n,)),
+        dma, dma, dma, dma, dma((3,)), dma((3,)), dma, dma,
+    ]
+    hbm = pl.BlockSpec(memory_space=pl.ANY)
+    shape = jax.ShapeDtypeStruct
+    outs = pl.pallas_call(
+        layer_kernel,
+        out_shape=(
+            shape(tokens.shape, BF),
+            shape(tokens.shape, F32),
+            shape(w_qkv.shape, F32),
+            shape(w_out.shape, F32),
+            shape(w_in.shape, F32),
+            shape(w_down.shape, F32),
+            shape((16, 256), F32),
+        ),
+        in_specs=[hbm, pl.BlockSpec(memory_space=pltpu.SMEM)] + [hbm] * 6,
+        out_specs=(hbm,) * 7,
+        scratch_shapes=scratch,
+        compiler_params=pltpu.CompilerParams(
+            collective_id=0, has_side_effects=True, vmem_limit_bytes=64 << 20
+        ),
+        name="layer",
+    )(tokens, lengths, w_qkv, w_out, w_in, w_down, segments, cotangent)
+    grad_vector = outs[6][:3, : norms_biases.shape[0] // 3].reshape(-1)
+    return (*outs[:6], grad_vector)
 
 
 def norm_rows(values, gain_row, shift_row):
@@ -289,4 +1157,7 @@
         P("wide", None),
         P("wide"),
     )
-    return jax.shard_map(local, mesh=mesh, in_specs=in_specs, out_specs=out_specs, check_vma=False)
+    chips = (ZS * YS * CS, 2)
+    fused = tuple(mesh.shape[axis] for axis in ("wide", "narrow")) == chips
+    step = fused_layer if fused else local
+    return jax.shard_map(step, mesh=mesh, in_specs=in_specs, out_specs=out_specs, check_vma=False)

time: 703 us -> 194 us (0.28); the launches traced: 695 us -> 193 us
  waiting for transfers between devices: 321 us -> 0 us
  Pallas kernels: 0 us -> 183 us
  matrix products: 146 us -> 0 us
  blocking collectives: 127 us -> 0 us
  other arithmetic: 39.4 us -> 0 us
  local copies, waits for them, and re-layouts: 43.9 us -> 9.25 us
  between operations: 16.1 us -> 1.31 us
    reduce_scatter x3 -> x0, waiting for transfers between devices: 216 us -> none  [the longest x1 79 us: local(): lax.psum_scatter(totals[3].astype(jnp.bfloat16), 'wide', scatter_dimensio...]
    pallas_call x0 -> x1, Pallas kernels: none -> 183 us  [fused_layer(): pl.pallas_call(layer_kernel, out_shape=(shape(tokens.shape, BF), shape(to...]
    dot_general x62 -> x0, matrix products: 141 us -> none  [the longest x2 37.9 us: layer_forward(): jnp.dot(activated, w_down, preferred_element_type=jnp.float32) + params[5]]
    unnamed x2 -> x0, blocking collectives: 122 us -> none
    all_gather x4 -> x0, waiting for transfers between devices: 57.9 us -> none  [the longest x1 33.1 us: local(): lax.all_gather(w_down, 'wide', axis=0, tiled=True)]
    unnamed x10 -> x0, waiting for transfers between devices: 47.6 us -> none
    unnamed x60 -> x16, local copies, waits for them, and re-layouts: 23.1 us -> 6.4 us
    reduce_sum x17 -> x0, other arithmetic: 13.6 us -> none  [the longest x2 3.02 us: norm_rows(): return centred * lax.rsqrt(spread + 1e-06) * gain_row + shift_row]
  transfers between devices with their start and end apart: 9 -> 0, of which waited for: 6 -> 0; matrix products, arithmetic and copies ran while one was open for 15% -> 0% of each run, Pallas kernels for 0% -> 0%
where the time goes in v1:
time: 194 us; the launch traced here: 193 us
  Pallas kernels  183 us (94%)
  local copies, waits for them, and re-layouts  9.25 us (5%)
    pallas_call x1, Pallas kernels, fused_layer(): pl.pallas_call(layer_kernel, out_shape=(shape(tokens.shape, BF), shape(to...  183 us
    unnamed x16, local copies, waits for them, and re-layouts  6.4 us

profile of v1, /device:TPU:0, one launch (start us, length us, event | category | flops | bytes accessed | tf_op | source)
XLA Modules:
  0.0 193.3 jit_solution(11207356573576859031)
XLA Ops:
  1.3 0.8 reshape.20
  2.0 0.6 pad.4.vec_hbm
  2.7 182.7 %layer.1 = (bf16[1,512,768]{2,1,0:T(8,128)(2,1)}, f32[1,512,768]{2,1,0:T(8,128)}, f32[48,2304]{1,0:T(8,128)}, f32[48,768]{1,0:T(8,128)}, f32[48,3072]{1,0:T(8,12...) custom-call(bf16[1,512,768]{2,1,0:T(8,128)(2,1)} %x_hbm.1, s32[1]{0:T(128)S(6)} %copy.21.len_ref, bf16[48,2304]{1,0:T(8,128)(2,1)} %wqkv_hbm.1, ...), custom_call_target="tpu_custom_call" | custom-call | tf_op jit(solution)/shard_map/layer/pallas_call | solution.py:854
  185.4 0.0 copy-start
  185.4 0.8 slice.3
  186.2 0.7 reshape.21
  186.9 2.1 %copy.22 = bf16[1,512,768]{2,1,0:T(8,128)(2,1)} copy(bf16[1,512,768]{2,1,0:T(8,128)(2,1)} %get-tuple-element.28) | data formatting | bytes 1572864
  188.9 0.0 copy-done
  188.9 0.0 copy-start.3
  188.9 0.0 copy-start.4
  188.9 0.0 copy-start.2
  188.9 1.1 copy.23
  190.1 0.1 copy-done.3
  190.2 0.0 copy-start.1
  190.2 0.8 copy.24
  191.0 0.0 copy-done.4
  191.0 0.7 copy.25
  191.6 0.0 copy-done.2
  191.6 0.8 copy.26
  192.5 0.0 copy-done.1
  192.5 0.8 copy.27
Async XLA Ops:
  185.4 3.6 %copy-start = (f32[1,512,768]{2,1,0:T(8,128)S(1)}, f32[1,512,768]{2,1,0:T(8,128)}, u32[]{:S(2)}) copy-start(f32[1,512,768]{2,1,0:T(8,128)} %get-tuple-element.29) | copy-start | bytes 4718596
  188.9 1.3 copy-start.3
  188.9 2.0 %copy-start.4 = (f32[48,768]{1,0:T(8,128)S(1)}, f32[48,768]{1,0:T(8,128)}, u32[]{:S(2)}) copy-start(f32[48,768]{1,0:T(8,128)} %get-tuple-element.31) | copy-start | bytes 442372
  188.9 2.7 %copy-start.2 = (f32[48,3072]{1,0:T(8,128)S(1)}, f32[48,3072]{1,0:T(8,128)}, u32[]{:S(2)}) copy-start(f32[48,3072]{1,0:T(8,128)} %get-tuple-element.32) | copy-start | bytes 1769476
  190.2 2.2 %copy-start.1 = (f32[192,768]{1,0:T(8,128)S(1)}, f32[192,768]{1,0:T(8,128)}, u32[]{:S(2)}) copy-start(f32[192,768]{1,0:T(8,128)} %get-tuple-element.33) | copy-start | bytes 1769476

commit v2 on v1

--- a/solution.py
+++ b/solution.py
@@ -17,6 +17,9 @@
 ZH, ZL, YS, CS = 2, 2, 2, 2
 ZS = ZH * ZL
 QKV, OUT, IN, DOWN, CHUNKS = 0, 3, 4, 8, 12
+CUTS = 1
+PARTS = CUTS * CHUNKS
+LAGS = (2, 1, 1, 1)
 SQRT_HALF = 0.7071067811865476
 INV_SQRT_TAU = 0.3989422804014327
 
@@ -45,13 +48,12 @@
     wa, wd, vb, gd, go, gv, rcore, rya, rxb, rza, ryb, rzb, rxa, rfb, rv_core, rv_y, rv_z, rv_x, fin, fv,
     x, cot, qkv, vt, pt, ct, n1, y1b, y1t, act, dact, h2, dfb, dcx, rs1, prm, vg,
     s_load, s_vload, s_io, s_store,
-    gsz, grz, gsy, gry, gsx1, grx1, gsx2, grx2, gsc, grc, vsz, vrz, vsy, vry, vsc, vrc,
-    rsc, rrc, rsya, rrya, rsxb, rrxb, rsza, rrza, rsyb, rryb, rszb, rrzb, rsxa, rrxa, rsfb, rrfb,
-    wsc, wrc, wsy, wry, wsz, wrz, wsx, wrx,
+    g_sent, grz, gry, grx, grc, v_sent, vrz, vry, vrc,
+    r_sent, rv_sent, rrc, rry, rrx, rrz, rrf, wrc, wry, wrz, wrx,
 ):
     seq, model = x.shape
     rows = wa.shape[-2]
-    hidden = act.shape[1]
+    hidden = dact.shape[1]
     pair = 2 * (model // HEADS)
     head = model // HEADS
     group = model // 3
@@ -84,42 +86,39 @@
 
     ALL = slice(None)
 
+    def drained(ref, sem):
+        pltpu.make_async_copy(ref, ref, sem).wait()
+
+    def rows_of(count):
+        return x.at[pl.ds(0, count), pl.ds(0, model // CUTS)]
+
     def wpiece(k, zz, yy, cc, r=ALL):
         zi = (ALL, ALL) if zz is None else (zz // ZL, lax.rem(zz, ZL))
         if k < DOWN:
             return wa.at[(k, *zi, yy, cc, r)]
         return wd.at[(*zi, yy, cc, k - DOWN, r)]
 
-    loads = []
-
     def load(src, dst, sem):
         cp = pltpu.make_async_copy(src, dst, sem)
         cp.start()
         return cp
 
-    own_loads = [[] for _ in range(CHUNKS)]
     load_vec = load(vec_hbm, vb.at[zh, zl, y, c], s_vload)
     load_x = load(x_hbm.at[0], x, s_io.at[0])
     for k in range(CHUNKS):
         if k < OUT:
             for part in range(3):
-                own_loads[k].append(
-                    load(
-                        wqkv_hbm.at[:, pl.ds(part * model + k * group, group)],
-                        wa.at[k, zh, zl, y, c, :, pl.ds(part * group, group)],
-                        s_load.at[k, part],
-                    )
+                load(
+                    wqkv_hbm.at[:, pl.ds(part * model + k * group, group)],
+                    wa.at[k, zh, zl, y, c, :, pl.ds(part * group, group)],
+                    s_load.at[k],
                 )
         elif k < IN:
-            own_loads[k].append(load(wout_hbm, wa.at[k, zh, zl, y, c], s_load.at[k, 0]))
+            load(wout_hbm, wa.at[k, zh, zl, y, c], s_load.at[k])
         elif k < DOWN:
-            own_loads[k].append(
-                load(win_hbm.at[:, pl.ds((k - IN) * model, model)], wa.at[k, zh, zl, y, c], s_load.at[k, 0])
-            )
+            load(win_hbm.at[:, pl.ds((k - IN) * model, model)], wa.at[k, zh, zl, y, c], s_load.at[k])
         else:
-            own_loads[k].append(
-                load(wdown_hbm.at[pl.ds((k - DOWN) * rows, rows)], wd.at[zh, zl, y, c, k - DOWN], s_load.at[k, 0])
-            )
+            load(wdown_hbm.at[pl.ds((k - DOWN) * rows, rows)], wd.at[zh, zl, y, c, k - DOWN], s_load.at[k])
     load_cot = load(cot_hbm.at[0], cot, s_io.at[1])
 
     barrier = pltpu.get_barrier_semaphore()
@@ -132,100 +131,99 @@
     given = pl.ds(pl.multiple_of(px * 2 * third, third), third)
     taken = pl.ds(pl.multiple_of((1 - px) * 2 * third, third), third)
 
-    def g_z(k, dz, source):
-        piece = wpiece(k, source, y, c, kept)
-        return remote(piece, piece, gsz.at[k, dz - 1], grz.at[k, dz - 1], device(ahead(dz), y, c, px))
-
-    def g_y(k, column):
-        piece = wpiece(k, None, column, c, kept)
-        return remote(piece, piece, gsy.at[k], gry.at[k], across_y)
-
-    def g_x1(k, dz, r):
-        piece = wpiece(k, behind(dz), y, c, r)
-        return remote(piece, piece, gsx1.at[k, dz - 1], grx1.at[k, dz - 1], across_x)
-
-    def g_x2(k, r):
-        piece = wpiece(k, None, 1 - y, c, r)
-        return remote(piece, piece, gsx2.at[k], grx2.at[k], across_x)
-
-    def g_core(k, core):
-        piece = wpiece(k, None, ALL, core)
-        return remote(piece, piece, gsc.at[k], grc.at[k], sibling)
+    def wcut(i, zz, yy, cc, r=ALL):
+        cols = pl.ds((i % CUTS) * (model // CUTS), model // CUTS)
+        k = i // CUTS
+        zi = (ALL, ALL) if zz is None else (zz // ZL, lax.rem(zz, ZL))
+        if k < DOWN:
+            return wa.at[(k, *zi, yy, cc, r, cols)]
+        return wd.at[(*zi, yy, cc, k - DOWN, r, cols)]
+
+    def g_z(i, dz, source):
+        piece = wcut(i, source, y, c, kept)
+        return remote(piece, piece, g_sent.at[i], grz.at[i], device(ahead(dz), y, c, px))
+
+    def g_y(i, dz, column):
+        piece = wcut(i, behind(dz), column, c, kept)
+        return remote(piece, piece, g_sent.at[i], gry.at[i], across_y)
+
+    def g_x1(i, dz, r):
+        piece = wcut(i, behind(dz), y, c, r)
+        return remote(piece, piece, g_sent.at[i], grx.at[i], across_x)
+
+    def g_x2(i, r):
+        piece = wcut(i, None, 1 - y, c, r)
+        return remote(piece, piece, g_sent.at[i], grx.at[i], across_x)
+
+    def g_core(i, core):
+        piece = wcut(i, None, ALL, core)
+        return remote(piece, piece, g_sent.at[i], grc.at[i], sibling)
 
     def v_z(dz, source):
         piece = vb.at[source // ZL, lax.rem(source, ZL), y, c]
-        return remote(piece, piece, vsz.at[dz - 1], vrz.at[dz - 1], device(ahead(dz), y, c, px))
+        return remote(piece, piece, v_sent, vrz, device(ahead(dz), y, c, px))
 
     def v_y(column):
         piece = vb.at[:, :, column, c]
-        return remote(piece, piece, vsy, vry, across_y)
+        return remote(piece, piece, v_sent, vry, across_y)
 
     def v_core(core):
         piece = vb.at[:, :, :, core]
-        return remote(piece, piece, vsc, vrc, sibling)
-
-    def e1(k):
-        if not 0 <= k < CHUNKS:
+        return remote(piece, piece, v_sent, vrc, sibling)
+
+    def e1(i):
+        if not 0 <= i < PARTS:
             return
-        for cp in own_loads[k]:
-            cp.wait()
-        if k == 0:
+        if i % CUTS == 0:
+            drained(x.at[pl.ds(0, rows)], s_load.at[i // CUTS])
+        if i == 0:
             load_vec.wait()
             for dz in (1, 2, 3):
                 v_z(dz, z).start()
         for dz in (1, 2, 3):
-            g_z(k, dz, z).start()
-
-    def e2(k):
-        if not 0 <= k < CHUNKS:
+            g_z(i, dz, z).start()
+        g_y(i, 0, y).start()
+
+    def e2(i):
+        if not 0 <= i < PARTS:
             return
-        if k == 0:
-            for dz in (1, 2, 3):
-                v_z(dz, behind(dz)).wait_recv()
+        if i == 0:
+            drained(rv_z, vrz)
             v_y(y).start()
+        drained(rows_of(3 * 2 * third), grz.at[i])
         for dz in (1, 2, 3):
-            g_z(k, dz, behind(dz)).wait_recv()
-        g_y(k, y).start()
-        for dz in (1, 2, 3):
-            g_x1(k, dz, given).start()
-
-    def e3(k):
-        if not 0 <= k < CHUNKS:
+            g_y(i, dz, y).start()
+            g_x1(i, dz, given).start()
+
+    def e3(i):
+        if not 0 <= i < PARTS:
             return
-        if k == 0:
+        if i == 0:
             v_y(1 - y).wait_recv()
             v_core(c).start()
-        g_y(k, 1 - y).wait_recv()
-        g_x2(k, given).start()
-
-    def e4(k):
-        if not 0 <= k < CHUNKS:
+        drained(rows_of(ZS * 2 * third), gry.at[i])
+        g_x2(i, given).start()
+
+    def e4(i):
+        if not 0 <= i < PARTS:
             return
-        for dz in (1, 2, 3):
-            g_x1(k, dz, taken).wait_recv()
-        g_x2(k, taken).wait_recv()
-        g_core(k, c).start()
-
-    def e5(k):
-        if not 0 <= k < CHUNKS:
+        drained(rows_of((ZS + ZS - 1) * third), grx.at[i])
+        g_core(i, c).start()
+
+    def e5(i):
+        if not 0 <= i < PARTS:
             return
-        if k == 0:
+        if i == 0:
             v_core(1 - c).wait_recv()
-        g_core(k, 1 - c).wait_recv()
+        g_core(i, 1 - c).wait_recv()
 
     def sent(k):
-        for dz in (1, 2, 3):
-            g_z(k, dz, z).wait_send()
-            g_x1(k, dz, given).wait_send()
-        g_y(k, y).wait_send()
-        g_x2(k, given).wait_send()
-        g_core(k, c).wait_send()
+        count = (3 + ZS) * 2 * third + (2 * ZS - 1) * third + ZS * YS * rows
+        for i in range(CUTS * k, CUTS * (k + 1)):
+            drained(qkv.at[:, pl.ds(0, count // 3), pl.ds(0, model // CUTS)], g_sent.at[i])
 
     def vec_sent():
-        for dz in (1, 2, 3):
-            v_z(dz, z).wait_send()
-        v_y(y).wait_send()
-        v_core(c).wait_send()
+        drained(x.at[pl.ds(0, 80)], v_sent)
 
     def place_matrix(k, lanes):
         i = lax.broadcasted_iota(jnp.int32, (lanes, model), 0)
@@ -311,24 +309,24 @@
         loop(seq // 128, tile)
 
     def feed_up(j):
-        def tile(i):
-            cols = span(i, 256)
-            wide_cols = pl.ds(pl.multiple_of(j * model + i * 256, 256), 256)
+        for t in range(2):
+            cols = slice(t * half, (t + 1) * half)
+            wide_cols = slice(j * model + t * half, j * model + (t + 1) * half)
             u = dot(y1b[...], weight(IN + j, cols)) + prm[8 + j : 9 + j, cols]
             phi = 0.5 * (1.0 + lax.erf(u * SQRT_HALF))
-            act[:, wide_cols] = (u * phi).astype(BF)
+            act[2 * j + t] = (u * phi).astype(BF).T.reshape(CS, 4, rows, seq)
             dact[:, wide_cols] = (phi + u * (jnp.exp(-0.5 * u * u) * INV_SQRT_TAU)).astype(BF)
 
-        loop(model // 256, tile)
-
-    def feed_down():
-        def tile(i):
-            cols = span(i, 256)
-            w = wd[:, :, :, :, :, :, cols].reshape(hidden, 256)
-            y1 = n1[:, cols] * prm[3:4, cols] + prm[4:5, cols]
-            h2[:, cols] = y1 + (dot(act[...], w) + prm[5:6, cols])
-
-        loop(model // 256, tile)
+    def act_rows(m):
+        return act[:, :, m].reshape(-1, seq)
+
+    def feed_down(m):
+        w = wd[:, :, :, :, m].reshape(-1, model)
+        part = dot(act_rows(m), w, TN)
+        if m == 0:
+            h2[...] = part + (n1[...] * prm[3:4, :] + prm[4:5, :]) + prm[5:6, :]
+        else:
+            h2[...] += part
 
     def vsum(row, value):
         vg[row : row + 1, :] += jnp.sum(value, axis=0, keepdims=True)
@@ -357,14 +355,8 @@
 
         loop(seq // 128, tile)
 
-    def grad_down():
-        def tile(i):
-            cols = span(i, 2 * 4 * rows)
-            g = dot(act[:, cols], dfb[...], TN).astype(BF).reshape(CS, 4, rows, model)
-            zz = i // YS
-            gd[zz // ZL, lax.rem(zz, ZL), lax.rem(i, YS)] = g
-
-        loop(ZS * YS, tile)
+    def grad_down(m):
+        gd[m] = dot(act_rows(m), dfb[...]).astype(BF).reshape(gd.shape[1:])
 
     def grad_act(j):
         def tile(t):
@@ -470,7 +462,7 @@
 
     def gpiece(k, zi, yy, cc, cols=ALL):
         if k < 4:
-            return gd.at[(*zi, yy, cc, k, ALL, cols)]
+            return gd.at[(k, *zi, yy, cc, ALL, cols)]
         if k < 8:
             return wd.at[(*zi, yy, cc, k - 4, ALL, cols)]
         if k < 9:
@@ -484,30 +476,30 @@
         return (zz // ZL, lax.rem(zz, ZL))
 
     def r_core(k):
-        return remote(gpiece(k, every, ALL, 1 - c), rcore.at[k], rsc.at[k], rrc.at[k], sibling)
+        return remote(gpiece(k, every, ALL, 1 - c), rcore.at[k], r_sent.at[k], rrc.at[k], sibling)
 
     def r_ya(k):
-        return remote(gpiece(k, every, 1 - y, c, left), rya.at[k], rsya.at[k], rrya.at[k], across_y)
+        return remote(gpiece(k, every, 1 - y, c, left), rya.at[k], r_sent.at[k], rry.at[k, 0], across_y)
 
     def r_xb(k):
-        return remote(gpiece(k, (ALL, 1 - px), ALL, c, right), rxb.at[k], rsxb.at[k], rrxb.at[k], across_x)
+        return remote(gpiece(k, (ALL, 1 - px), ALL, c, right), rxb.at[k], r_sent.at[k], rrx.at[k, 0], across_x)
 
     def r_za(k, dz):
         piece = gpiece(k, at_z(ahead(dz)), y, c, left)
-        return remote(piece, rza.at[k, dz - 1], rsza.at[k, dz - 1], rrza.at[k, dz - 1], device(ahead(dz), y, c, px))
+        return remote(piece, rza.at[k, dz - 1], r_sent.at[k], rrz.at[k, 0], device(ahead(dz), y, c, px))
 
     def r_yb(k):
-        return remote(gpiece(k, (ALL, px), 1 - y, c, right), ryb.at[k], rsyb.at[k], rryb.at[k], across_y)
+        return remote(gpiece(k, (ALL, px), 1 - y, c, right), ryb.at[k], r_sent.at[k], rry.at[k, 1], across_y)
 
     def r_xa(k):
-        return remote(gpiece(k, mine, y, c, left), rxa.at[k], rsxa.at[k], rrxa.at[k], across_x)
+        return remote(gpiece(k, mine, y, c, left), rxa.at[k], r_sent.at[k], rrx.at[k, 1], across_x)
 
     def r_zb(k, dz):
         piece = gpiece(k, at_z(ahead(dz)), y, c, right)
-        return remote(piece, rzb.at[k, dz - 1], rszb.at[k, dz - 1], rrzb.at[k, dz - 1], device(ahead(dz), y, c, px))
+        return remote(piece, rzb.at[k, dz - 1], r_sent.at[k], rrz.at[k, 1], device(ahead(dz), y, c, px))
 
     def r_fb(k):
-        return remote(gpiece(k, mine, y, c, right), rfb.at[k], rsfb.at[k], rrfb.at[k], across_x)
+        return remote(gpiece(k, mine, y, c, right), rfb.at[k], r_sent.at[k], rrf.at[k], across_x)
 
     same = zl == px
 
@@ -530,7 +522,7 @@
         if n_chunk(k):
             r_core(k).start()
         if k == CHUNKS - 1:
-            remote(gv.at[:, :, :, 1 - c], rv_core, wsc, wrc, sibling).start()
+            remote(gv.at[:, :, :, 1 - c], rv_core, rv_sent, wrc, sibling).start()
 
     def r1(k):
         if not n_chunk(k):
@@ -545,18 +537,18 @@
         r_ya(k).start()
         r_xb(k).start()
         if k == CHUNKS - 1:
-            remote(gv.at[:, :, :, 1 - c], rv_core, wsc, wrc, sibling).wait_recv()
+            remote(gv.at[:, :, :, 1 - c], rv_core, rv_sent, wrc, sibling).wait_recv()
             add_into(gv.at[:, :, :, c], rv_core)
-            remote(gv.at[:, :, 1 - y, c], rv_y, wsy, wry, across_y).start()
+            remote(gv.at[:, :, 1 - y, c], rv_y, rv_sent, wry, across_y).start()
 
     def v_rz(dz):
         return remote(
-            gv.at[(*at_z(ahead(dz)), y, c)], rv_z.at[dz - 1], wsz.at[dz - 1], wrz.at[dz - 1],
+            gv.at[(*at_z(ahead(dz)), y, c)], rv_z.at[dz - 1], rv_sent, wrz,
             device(ahead(dz), y, c, px),
         )
 
     def v_rx():
-        return remote(gv.at[(*mine, y, c)], rv_x, wsx, wrx, across_x)
+        return remote(gv.at[(*mine, y, c)], rv_x, rv_sent, wrx, across_x)
 
     def r2(k):
         if not n_chunk(k):
@@ -569,7 +561,7 @@
         add_into(gpiece(k, (ALL, px), ALL, c, right), rxb.at[k])
         r_yb(k).start()
         if k == CHUNKS - 1:
-            remote(gv.at[:, :, 1 - y, c], rv_y, wsy, wry, across_y).wait_recv()
+            remote(gv.at[:, :, 1 - y, c], rv_y, rv_sent, wry, across_y).wait_recv()
             add_into(gv.at[:, :, y, c], rv_y)
             for dz in (1, 2, 3):
                 v_rz(dz).start()
@@ -581,13 +573,11 @@
         add_into(gpiece(k, (ALL, px), y, c, right), ryb.at[k])
         for dz in (1, 2, 3):
             to_parity(dz, lambda dz=dz: r_zb(k, dz).start())
-        for dz in (1, 2, 3):
-            r_za(k, dz).wait_recv()
+        drained(rza.at[k], rrz.at[k, 0])
         add_into(gpiece(k, mine, y, c, left), rza.at[k, 0], rza.at[k, 1], rza.at[k, 2])
         r_xa(k).start()
         if k == CHUNKS - 1:
-            for dz in (1, 2, 3):
-                v_rz(dz).wait_recv()
+            drained(rv_z, wrz)
             add_into(gv.at[(*mine, y, c)], rv_z.at[0], rv_z.at[1], rv_z.at[2])
             v_rx().start()
 
@@ -597,8 +587,7 @@
 
         @pl.when(same)
         def _():
-            for dz in (1, 2, 3):
-                r_zb(k, dz).wait_recv()
+            drained(rzb.at[k], rrz.at[k, 1])
             add_into(gpiece(k, mine, y, c, right), rzb.at[k, 0], rzb.at[k, 1], rzb.at[k, 2])
             r_fb(k).start()
             fin[k, :, right] = gpiece(k, mine, y, c, right)[...].astype(F32)
@@ -609,12 +598,10 @@
             v_rx().wait_recv()
             fv[...] = gv[(*mine, y, c)].astype(F32) + rv_x[...].astype(F32)
 
-    stores = []
-
-    def store(src, dst):
-        cp = pltpu.make_async_copy(src, dst, s_store.at[len(stores)])
+    def store(src, dst, i=0):
+        cp = pltpu.make_async_copy(src, dst, s_store.at[i])
         cp.start()
-        stores.append(cp)
+        return cp
 
     def r5(k):
         if not n_chunk(k):
@@ -639,21 +626,9 @@
                 )
 
     def sums_sent(k):
-        r_core(k).wait_send()
-        r_ya(k).wait_send()
-        r_xb(k).wait_send()
-        r_yb(k).wait_send()
-        r_xa(k).wait_send()
-        for dz in (1, 2, 3):
-            r_za(k, dz).wait_send()
-            to_parity(dz, lambda dz=dz: r_zb(k, dz).wait_send())
-        pl.when(same)(lambda: r_fb(k).wait_send())
+        drained(wa.at[0], r_sent.at[k])
 
     vg[...] = jnp.zeros_like(vg)
-    e1(0)
-    e1(1)
-    load_x.wait()
-
     def forward(k):
         if k < 0:
             return
@@ -666,20 +641,28 @@
             out_proj()
         elif k < DOWN:
             feed_up(k - IN)
-
-    for t in range(1, CHUNKS + 4):
-        e5(t - 4)
-        e4(t - 3)
-        e3(t - 2)
-        e2(t - 1)
-        e1(t + 1)
-        forward(t - 4)
+        else:
+            feed_down(k - DOWN)
+
+    lead, lag_y, lag_x, lag_c = LAGS
+    for i in range(lead):
+        e1(i)
+    load_x.wait()
+    last = PARTS + lag_y + lag_x + lag_c
+    for t in range(last):
+        e2(t)
+        e1(t + lead)
+        e3(t - lag_y)
+        e4(t - lag_y - lag_x)
+        done = t - lag_y - lag_x - lag_c
+        e5(done)
+        if done % CUTS == CUTS - 1:
+            forward(done // CUTS)
     load_cot.wait()
-    feed_down()
     norm_two()
-    store(dcx, out_hbm.at[0])
-    grad_down()
+    store_out = store(dcx, out_hbm.at[0], 1)
     for k in range(4):
+        grad_down(k)
         r0(k)
     r1(0)
     grad_act(0)
@@ -725,7 +708,7 @@
     r3(4)
     r4(3)
     r5(2)
-    stores[0].wait()
+    store_out.wait()
     grad_out()
     r0(8)
     grad_context()
@@ -763,7 +746,7 @@
     r5(6)
     r1(11)
     grad_x()
-    store(n1, gtok_hbm.at[0])
+    store_x = store(n1, gtok_hbm.at[0], 2)
     r2(10)
     r3(9)
     r4(8)
@@ -776,7 +759,7 @@
     r4(10)
     r5(9)
     r4(11)
-    store(fv, gvec_hbm)
+    store_vec = store(fv, gvec_hbm, 3)
     r5(10)
     r5(11)
     for k in range(IN):
@@ -784,13 +767,35 @@
     vec_sent()
     for k in range(CHUNKS):
         sums_sent(k)
-    remote(gv.at[:, :, :, 1 - c], rv_core, wsc, wrc, sibling).wait_send()
-    remote(gv.at[:, :, 1 - y, c], rv_y, wsy, wry, across_y).wait_send()
-    for dz in (1, 2, 3):
-        v_rz(dz).wait_send()
-    v_rx().wait_send()
-    for cp in stores[1:]:
-        cp.wait()
+    drained(gv, rv_sent)
+    drained(fin, s_store.at[0])
+    store_vec.wait()
+    store_x.wait()
+
+
+def place_kernel(cuts, *refs):
+    count = len(cuts)
+    sources, targets, held = refs[:count], refs[count : 2 * count], refs[2 * count : 3 * count]
+    sem_in, sem_out = refs[3 * count :]
+    moves = []
+    for src, dst, mid, parts in zip(sources, targets, held, cuts):
+        size = src.shape[-2] // parts
+        for j in range(parts):
+            at = (slice(None),) * (len(src.shape) - 2) + (pl.ds(j * size, size),)
+            i = len(moves)
+            moves.append(
+                (
+                    pltpu.make_async_copy(src.at[at], mid.at[at], sem_in.at[i]),
+                    pltpu.make_async_copy(mid.at[at], dst.at[at], sem_out.at[i]),
+                )
+            )
+    for first, _ in moves:
+        first.start()
+    for first, second in moves:
+        first.wait()
+        second.start()
+    for _, second in moves:
+        second.wait()
 
 
 def fused_layer(tokens, lengths, w_qkv, w_out, w_in, w_down, norms_biases, cotangent):
@@ -802,12 +807,12 @@
     segments = jnp.pad(norms_biases.reshape(3, -1), ((0, 13), (0, 256 - norms_biases.shape[0] // 3)))
     vm, dma = pltpu.VMEM, pltpu.SemaphoreType.DMA
     grid = (ZH, ZL, YS, CS)
-    n = CHUNKS
+    n, m = CHUNKS, PARTS
     scratch = [
         vm((DOWN, *grid, rows, model), BF),
         vm((*grid, 4, rows, model), BF),
         vm((*grid, 16, 256), BF),
-        vm((*grid, 4, rows, model), BF),
+        vm((4, *grid, rows, model), BF),
         vm((1, *grid, rows, model), BF),
         vm((*grid, 16, 256), BF),
         vm((n, ZH, ZL, YS, rows, model), BF),
@@ -833,7 +838,7 @@
         vm((seq, model), F32),
         vm((seq, model), BF),
         vm((model, seq), BF),
-        vm((seq, hidden), BF),
+        vm((ZS * YS, CS, 4, rows, seq), BF),
         vm((seq, hidden), BF),
         vm((seq, model), F32),
         vm((seq, model), BF),
@@ -841,13 +846,9 @@
         vm((seq, 1), F32),
         vm((16, model), F32),
         vm((16, model), F32),
-        dma((n, 3)), dma, dma((2,)), dma((21,)),
-        dma((n, 3)), dma((n, 3)), dma((n,)), dma((n,)), dma((n, 3)), dma((n, 3)),
-        dma((n,)), dma((n,)), dma((n,)), dma((n,)),
-        dma((3,)), dma((3,)), dma, dma, dma, dma,
-        dma((n,)), dma((n,)), dma((n,)), dma((n,)), dma((n,)), dma((n,)), dma((n, 3)), dma((n, 3)),
-        dma((n,)), dma((n,)), dma((n, 3)), dma((n, 3)), dma((n,)), dma((n,)), dma((n,)), dma((n,)),
-        dma, dma, dma, dma, dma((3,)), dma((3,)), dma, dma,
+        dma((n,)), dma, dma((2,)), dma((4,)),
+        dma((m,)), dma((m,)), dma((m,)), dma((m,)), dma((m,)), dma, dma, dma, dma,
+        dma((n,)), dma, dma((n,)), dma((n, 2)), dma((n, 2)), dma((n, 2)), dma((n,)), dma, dma, dma, dma,
     ]
     hbm = pl.BlockSpec(memory_space=pl.ANY)
     shape = jax.ShapeDtypeStruct
@@ -871,7 +872,16 @@
         name="layer",
     )(tokens, lengths, w_qkv, w_out, w_in, w_down, segments, cotangent)
     grad_vector = outs[6][:3, : norms_biases.shape[0] // 3].reshape(-1)
-    return (*outs[:6], grad_vector)
+    cuts = (2, 4, 1, 1, 1, 1)
+    placed = pl.pallas_call(
+        functools.partial(place_kernel, cuts),
+        out_shape=tuple(shape(o.shape, o.dtype) for o in outs[:6]),
+        in_specs=[hbm] * 6,
+        out_specs=(hbm,) * 6,
+        scratch_shapes=[vm(o.shape, o.dtype) for o in outs[:6]] + [dma((sum(cuts),)), dma((sum(cuts),))],
+        name="place",
+    )(*outs[:6])
+    return (*placed, grad_vector)
 
 
 def norm_rows(values, gain_row, shift_row):

time: 194 us -> 161 us (0.83)
  Pallas kernels: 183 us -> 157 us
  local copies, waits for them, and re-layouts: 9.25 us -> 2.74 us
    pallas_call x1, Pallas kernels: 183 us -> 153 us  [fused_layer(): pl.pallas_call(layer_kernel, out_shape=(shape(tokens.shape, BF), shape(to...]
    unnamed x16 -> x0, local copies, waits for them, and re-layouts: 6.4 us -> none
    pallas_call x0 -> x1, Pallas kernels: none -> 3.69 us  [fused_layer(): pl.pallas_call(functools.partial(place_kernel, cuts), out_shape=tuple((sh...]
where the time goes in v2:
time: 161 us
  Pallas kernels  157 us (98%)
  local copies, waits for them, and re-layouts  2.74 us (2%)
    pallas_call x1, Pallas kernels, fused_layer(): pl.pallas_call(layer_kernel, out_shape=(shape(tokens.shape, BF), shape(to...  153 us
    pallas_call x1, Pallas kernels, fused_layer(): pl.pallas_call(functools.partial(place_kernel, cuts), out_shape=tuple((sh...  3.69 us

profile of v2, /device:TPU:0, one launch (start us, length us, event | category | flops | bytes accessed | tf_op | source)
XLA Modules:
  0.0 160.7 jit_solution(14263899196941794007)
XLA Ops:
  1.3 0.8 reshape.20
  2.0 0.6 pad.4.vec_hbm
  2.7 152.9 %layer.1 = (bf16[1,512,768]{2,1,0:T(8,128)(2,1)}, f32[1,512,768]{2,1,0:T(8,128)}, f32[48,2304]{1,0:T(8,128)}, f32[48,768]{1,0:T(8,128)}, f32[48,3072]{1,0:T(8,12...) custom-call(bf16[1,512,768]{2,1,0:T(8,128)(2,1)} %x_hbm.1, s32[1]{0:T(128)S(6)} %copy.15.len_ref, bf16[48,2304]{1,0:T(8,128)(2,1)} %wqkv_hbm.1, ...), custom_call_target="tpu_custom_call" | custom-call | tf_op jit(solution)/shard_map/layer/pallas_call | solution.py:855
  155.6 3.7 %place.1 = (bf16[1,512,768]{2,1,0:T(8,128)(2,1)}, f32[1,512,768]{2,1,0:T(8,128)}, f32[48,2304]{1,0:T(8,128)}, f32[48,768]{1,0:T(8,128)}, f32[48,3072]{1,0:T(8,128)}, /*index=5*/f32[192,768]{1,0:T(8,128)}) custom-call(bf16[1,512,768]{2,1,0:T(8,128)(2,1)} %get-tuple-element.20.refs_0_, f32[1,512,768]{2,1,0:T(8,128)} %get-tuple-element.21.refs_1_, ...), custom_call_target="tpu_custom_call" | custom-call | tf_op jit(solution)/shard_map/place/pallas_call | solution.py:876
  159.3 0.7 slice.3
  160.0 0.7 reshape.21
